TPU v7x, 32 devices: a whole 2x2x4 slice. The times are simulated.
32 devices in a mesh: sx: 8 (over y, x, core), sy: 4 (over z).
Axes of the slice: x: 2, y: 2, z: 4, core: 2. Of those that a mesh axis runs over, the one named last changes fastest.
Arguments:
- schur_diag: bfloat16 [4, 8, 4, 512, 512], P('sy', 'sx'), may hold values from 0 to 17, as said below
- coupling: bfloat16 [4, 8, 3, 512, 512], P('sy', 'sx'), may hold values from 0 to 4
- right_side: float32 [4, 8, 4, 512], P('sy', 'sx'), may hold values from -12 to 12
- face_link: int32 [4, 8, 4], P('sy', 'sx'), may hold values from 0 to 1, as said below
- face_start: int32 [4, 8, 4], P('sy', 'sx'), may hold values from 0 to 1536, as said below
Outputs:
- solution_field: float32 [4, 8, 4, 512], P('sy', 'sx')
- residual: float32 [4, 8, 4, 512], P('sy', 'sx')
Inputs may be any that keep to these rules, and one draw needn't show every extreme that they name: `face_link`: Symmetric: a subdomain has a face toward a neighbour exactly when that neighbour has the face back; no face points out of the grid; some subdomain has all four faces. `face_start`: the four entries of a subdomain are 512 times a permutation of 0, 1, 2, 3. Symmetric blocks; each subdomain's whole panel matrix, with schur_diag on the block diagonal and coupling and its transpose beside it, is positive definite.
All inputs are finite; a program needn't handle non-finite values.
Results may differ from a plain program's by a relative error of at most 0.0004.
Values may be sent and summed in bfloat16 or wider, within the bound.
A program may use at most 64 MiB of HBM per device.

v0:
```python
import jax
import jax.numpy as jnp
from jax import lax
from jax.sharding import PartitionSpec as P

F = 512
SLOTS = 4
ITERS = 2


highest = lax.Precision.HIGHEST


def extended(shard, sides, width):
    for axis, dim in sides:
        devices, length = (lax.axis_size(axis), shard.shape[dim])
        up = [(i, (i + 1) % devices) for i in range(devices - 1)]
        down = [(j, i) for i, j in up]
        last = lax.slice_in_dim(shard, length - width, length, axis=dim)
        initial = lax.slice_in_dim(shard, 0, width, axis=dim)
        before = lax.ppermute(last, axis, up)
        after = lax.ppermute(initial, axis, down)
        shard = jnp.concatenate([before, shard, after], axis=dim)
    return shard


def inverse_slots(slot_ids):
    numbers = jnp.arange(SLOTS, dtype=jnp.int32)
    matched = slot_ids[..., :, None] == numbers
    return jnp.sum(jnp.where(matched, numbers[:, None], 0), axis=-2)


def panel_terms(blocks, coupling, vectors, with_diag):
    linked = coupling.astype(jnp.float32)
    upward = jnp.einsum("...pij,...pj->...pi", linked, vectors[..., 1:, :], precision=highest)
    downward = jnp.einsum("...pji,...pj->...pi", linked, vectors[..., :-1, :], precision=highest)
    border = jnp.zeros_like(vectors[..., :1, :])
    totals = jnp.concatenate([upward, border], axis=-2) + jnp.concatenate(
        [border, downward], axis=-2
    )
    if with_diag:
        totals = (
            jnp.einsum(
                "...pij,...pj->...pi", blocks.astype(jnp.float32), vectors, precision=highest
            )
            + totals
        )
    return totals


def solve_factor(factors, vectors):
    middle = jax.scipy.linalg.solve_triangular(factors, vectors[..., None], lower=True)
    return jax.scipy.linalg.solve_triangular(factors, middle, lower=True, trans=1)[..., 0]


def trade_vectors(values):
    along_x = extended(values[0:2], (("sx", 0),), 1)
    along_y = extended(values[2:4], (("sy", 0),), 1)
    return jnp.stack([along_x[0], along_x[3], along_y[0], along_y[3]])


def residual_dot(residual, precond_res):
    return lax.psum(0.5 * jnp.sum(residual * precond_res), ("sx", "sy"))


def body(schur_diag, coupling, right_side, face_link, face_start):
    blocks = schur_diag[0, 0]
    linked = coupling[0, 0]
    source = right_side[0, 0]
    slot_ids = face_start[0, 0] // F
    inverse = inverse_slots(slot_ids)
    alive = (face_link[0, 0] > 0)[:, None]
    alive_blocks = alive[:, :, None]
    identity = jnp.eye(F, dtype=jnp.float32)
    own_blocks = jnp.take(blocks, slot_ids, axis=0)
    along_x = extended(own_blocks[0:2], (("sx", 0),), 1)
    along_y = extended(own_blocks[2:4], (("sy", 0),), 1)
    partner = jnp.stack([along_x[0], along_x[3], along_y[0], along_y[3]])
    summed = own_blocks.astype(jnp.float32) + partner.astype(jnp.float32)
    factors = jnp.linalg.cholesky(jnp.where(alive_blocks, summed, identity))

    def assemble(values):
        return jnp.where(alive, values + trade_vectors(values), 0.0)

    def local_term(values, with_diag):
        panel = jnp.take(jnp.where(alive, values, 0.0), inverse, axis=0)
        terms = panel_terms(blocks, linked, panel, with_diag)
        return jnp.where(alive, jnp.take(terms, slot_ids, axis=0), 0.0)

    def precondition(values):
        first_solve = solve_factor(factors, values)
        spread = assemble(local_term(first_solve, False))
        return jnp.where(alive, solve_factor(factors, values - spread), 0.0)

    residual = assemble(source)
    solution = jnp.zeros_like(residual)
    precond_res = precondition(residual)
    direction = precond_res
    current = residual_dot(residual, precond_res)
    for iteration in range(ITERS):
        image = assemble(local_term(direction, True))
        alpha_step = current / lax.psum(0.5 * jnp.sum(direction * image), ("sx", "sy"))
        solution = solution + alpha_step * direction
        residual = residual - alpha_step * image
        if iteration + 1 < ITERS:
            precond_res = precondition(residual)
            following = residual_dot(residual, precond_res)
            direction = precond_res + following / current * direction
            current = following
    return (solution[None, None], residual[None, None])


def solution(mesh):
    return jax.shard_map(
        body,
        mesh=mesh,
        in_specs=(
            P("sy", "sx", None, None, None),
            P("sy", "sx", None, None, None),
            P("sy", "sx", None, None),
            P("sy", "sx", None),
            P("sy", "sx", None),
        ),
        out_specs=(P("sy", "sx", None, None), P("sy", "sx", None, None)),
        check_vma=False,
    )
```

profile of v0, /device:TPU:0, one launch (start us, length us, event | category | flops | bytes accessed | tf_op | source)
XLA Modules:
  0.0 842.3 jit_solution(7597123347309298912)
XLA Ops:
  4.3 4.2 copy.38
  11.7 3.2 collective-permute-start.4
  16.2 5.1 collective-permute-start.6
  22.6 3.2 collective-permute-start
  27.9 3.2 collective-permute-done.1
  31.1 4.5 collective-permute-start.2
  38.2 4.4 collective-permute-done.3
  42.8 4.0 add_select_fusion
  46.8 5.2 copy.39
  52.0 4.0 fusion
  58.0 46.9 %custom-call.37 = f32[4,128,128]{2,1,0:T(8,128)S(1)} custom-call(f32[4,128,128]{2,1,0:T(8,128)S(1)} %cholesky.274), custom_call_target="Cholesky" | custom-call | tf_op jit(solution)/shard_map/jit(cholesky)/cholesky | solution.py:80
  104.9 39.9 %custom-call.38 = f32[4,1,128,128]{2,3,1,0:T(8,128)} custom-call(f32[4,1,128,128]{3,2,1,0:T(8,128)S(1)} %select_bitcast_fusion.2), custom_call_target="InvertDiagBlocksLowerTriangular" | custom-call | tf_op jit(solution)/shard_map/jit(cholesky)/cholesky | solution.py:80
  153.3 47.1 %custom-call.39 = f32[4,128,128]{2,1,0:T(8,128)S(1)} custom-call(f32[4,128,128]{2,1,0:T(8,128)S(1)} %cholesky.278), custom_call_target="Cholesky" | custom-call | tf_op jit(solution)/shard_map/jit(cholesky)/cholesky | solution.py:80
  201.1 39.3 %custom-call.40 = f32[4,1,128,128]{2,3,1,0:T(8,128)S(1)} custom-call(f32[4,1,128,128]{3,2,1,0:T(8,128)S(1)} %get-tuple-element.96), custom_call_target="InvertDiagBlocksLowerTriangular" | custom-call | tf_op jit(solution)/shard_map/jit(cholesky)/cholesky | solution.py:80
  246.4 48.3 %custom-call.41 = f32[4,128,128]{2,1,0:T(8,128)} custom-call(f32[4,128,128]{2,1,0:T(8,128)} %cholesky.283), custom_call_target="Cholesky" | custom-call | tf_op jit(solution)/shard_map/jit(cholesky)/cholesky | solution.py:80
  296.5 41.1 %custom-call.42 = f32[4,1,128,128]{2,3,1,0:T(8,128)} custom-call(f32[4,1,128,128]{3,2,1,0:T(8,128)} %get-tuple-element.94), custom_call_target="InvertDiagBlocksLowerTriangular" | custom-call | tf_op jit(solution)/shard_map/jit(cholesky)/cholesky | solution.py:80
  342.3 46.9 %custom-call.43 = f32[4,128,128]{2,1,0:T(8,128)S(1)} custom-call(f32[4,128,128]{2,1,0:T(8,128)S(1)} %slice_subtract_fusion.2), custom_call_target="Cholesky" | custom-call | tf_op jit(solution)/shard_map/jit(cholesky)/cholesky | solution.py:80
  391.4 4.9 select_select_fusion
  396.3 15.1 %while.16 = (s32[]{:T(128)}, f32[4,512,512]{2,1,0:T(8,128)}, s32[4,2]{0,1:T(2,128)S(1)}, f32[4,4,128,128]{3,2,0,1:T(8,128)}, s32[]{:T(128)}) while((s32[]{:T(128)}, f32[4,512,512]{2,1,0:T(8,128)}, s32[4,2]{0,1:T(2,128)S(1)}, f32[4,4,128,128]{3,2,0,1:T(8,128)}, s32[]{:T(128)}) %tuple.84), condition=%wide.while_cond.1.clone, body=%wide.while_body.1.clone.sunk | while | flops 2 | bytes 525921 | solution.py:53
  397.0 3.2 bitcast_dynamic-update-slice_fusion.2
  411.4 158.2 %custom-call.53 = f32[4,4,128,128]{2,3,1,0:T(8,128)S(1)} custom-call(f32[4,4,128,128]{3,2,1,0:T(8,128)} %bitcast.787), custom_call_target="InvertDiagBlocksLowerTriangular" | custom-call | tf_op jit(solution)/shard_map/jit(_solve_triangular)/vmap()/triangular_solve | solution.py:53
  589.1 3.9 collective-permute-start.10
  598.5 3.2 collective-permute-done.9
  623.1 4.3 collective-permute-start.12
  628.7 4.5 collective-permute-start.14
  634.6 4.1 collective-permute-done.15
  640.7 42.7 %all-reduce.9 = (f32[]{:T(128)}, f32[]{:T(128)}) all-reduce(f32[]{:T(128)S(6)} %mul.80, f32[]{:T(128)S(6)} %mul.82), channel_id=1, replica_groups=mesh['sx'=8,'sy'=4] {'sx','sy'}, use_global_device_ids=true, to_apply=%region_10.14 | all-reduce | flops 2 | bytes 16 | tf_op jit(solution)/shard_map/psum | solution.py:63
  711.4 4.1 collective-permute-done.19
  730.3 44.1 %psum.30 = f32[]{:T(128)} all-reduce(f32[]{:T(128)S(6)} %mul.88), channel_id=1, replica_groups=mesh['sx'=8,'sy'=4] {'sx','sy'}, use_global_device_ids=true, to_apply=%region_14.18 | all-reduce | flops 1 | bytes 8 | tf_op jit(solution)/shard_map/psum | solution.py:63
  786.3 3.3 collective-permute-start.22
  790.9 4.1 collective-permute-done.23
  796.4 42.8 %psum.31 = f32[]{:T(128)} all-reduce(f32[]{:T(128)S(6)} %mul.92), channel_id=1, replica_groups=mesh['sx'=8,'sy'=4] {'sx','sy'}, use_global_device_ids=true, to_apply=%region_16.20 | all-reduce | flops 1 | bytes 8 | tf_op jit(solution)/shard_map/psum | solution.py:102
  (261 shorter events, 155.7 us)
Async XLA Ops:
  0.6 1.6 copy-start
  8.4 14.1 %copy-start.4 = (f32[1,1,4,512]{3,2,1,0:T(4,128)S(1)}, f32[1,1,4,512]{3,2,1,0:T(4,128)}, u32[]{:S(2)}) copy-start(f32[1,1,4,512]{3,2,1,0:T(4,128)} %param.13) | copy-start | bytes 24580
  8.4 17.7 %copy-start.7 = (s32[1,1,4]{2,1,0:T(1,128)S(1)}, s32[1,1,4]{2,1,0:T(1,128)}, u32[]{:S(2)}) copy-start(s32[1,1,4]{2,1,0:T(1,128)} %param.14) | copy-start | bytes 52
  11.7 31.0 %collective-permute-start.4 = (bf16[1,512,512]{1,2,0:T(8,128)(2,1)}, bf16[1,512,512]{1,2,0:T(8,128)(2,1)}, u32[]{:S(2)}, u32[]{:S(2)}) collective-permute-start(bf16[1,512,512]{1,2,0:T(8,128)(2,1)} %get-tuple-element.89), channel_id=1, source_target_pairs={{0,4},{4,8},{8,12},{12,16},{16,20},{20,24},{24,28},{1,5},{5,9},{9,... | collective-permute-start | bytes 1572872 | tf_op jit(solution)/shard_map/ppermute | solution.py:21
  14.9 27.9 %collective-permute-start.5 = (bf16[1,512,512]{1,2,0:T(8,128)(2,1)}, bf16[1,512,512]{1,2,0:T(8,128)(2,1)}, u32[]{:S(2)}, u32[]{:S(2)}) collective-permute-start(bf16[1,512,512]{1,2,0:T(8,128)(2,1)} %get-tuple-element.92), channel_id=1, source_target_pairs={{4,0},{8,4},{12,8},{16,12},{20,16},{24,20},{28,24},{5,1},{9,5},{13... | collective-permute-start | bytes 1572872 | tf_op jit(solution)/shard_map/ppermute | solution.py:22
  16.2 26.6 %collective-permute-start.6 = (bf16[1,512,512]{1,2,0:T(8,128)(2,1)}, bf16[1,512,512]{1,2,0:T(8,128)(2,1)}, u32[]{:S(2)}, u32[]{:S(2)}) collective-permute-start(bf16[1,512,512]{1,2,0:T(8,128)(2,1)} %get-tuple-element.91), channel_id=1, source_target_pairs={{0,1},{1,2},{2,3},{4,5},{5,6},{6,7},{8,9},{9,10},{10,11},{12,13},{... | collective-permute-start | bytes 1572872 | tf_op jit(solution)/shard_map/ppermute | solution.py:21
  21.3 21.5 %collective-permute-start.7 = (bf16[1,512,512]{1,2,0:T(8,128)(2,1)}, bf16[1,512,512]{1,2,0:T(8,128)(2,1)}, u32[]{:S(2)}, u32[]{:S(2)}) collective-permute-start(bf16[1,512,512]{1,2,0:T(8,128)(2,1)} %get-tuple-element.90), channel_id=1, source_target_pairs={{1,0},{2,1},{3,2},{5,4},{6,5},{7,6},{9,8},{10,9},{11,10},{13,12},{... | collective-permute-start | bytes 1572872 | tf_op jit(solution)/shard_map/ppermute | solution.py:22
  22.6 4.0 collective-permute-start
  26.6 4.5 collective-permute-start.1
  31.1 5.8 collective-permute-start.2
  36.9 5.7 collective-permute-start.3
  42.7 4.0 copy-start.5
  56.0 1.9 copy-start.1
  144.9 2.5 copy-start.3
  391.3 178.2 %slice-start = ((f32[4,512,1]{1,0,2:T(4,128)}), f32[4,128,1]{1,0,2:T(4,128)S(1)}, s32[]{:S(2)}) async-start(f32[4,512,1]{1,0,2:T(4,128)} %copy-done.5), calls=%async_computation | async-start | bytes 4096 | tf_op jit(solution)/shard_map/jit(_solve_triangular)/vmap()/triangular_solve | solution.py:52
  391.3 180.1 %copy-start.6 = (f32[4,512,1]{1,0,2:T(4,128)S(1)}, f32[4,512,1]{1,0,2:T(4,128)}, u32[]{:S(2)}) copy-start(f32[4,512,1]{1,0,2:T(4,128)} %copy-done.5) | copy-start | bytes 24580
  589.1 9.2 %collective-permute-start.10 = (f32[1,512]{1,0:T(1,128)S(1)}, f32[1,512]{1,0:T(1,128)S(1)}, u32[]{:S(2)}, u32[]{:S(2)}) collective-permute-start(f32[1,512]{1,0:T(1,128)S(1)} %get-tuple-element.118), channel_id=1, source_target_pairs={{0,1},{1,2},{2,3},{4,5},{5,6},{6,7},{8,9},{9,10},{10,11},{12,13},{... | collective-permute-start | bytes 6152 | tf_op jit(solution)/shard_map/ppermute | solution.py:21
  593.0 5.5 collective-permute-start.11
  594.3 4.2 collective-permute-start.8
  597.0 4.8 collective-permute-start.9
  623.1 11.4 %collective-permute-start.12 = (f32[1,512]{1,0:T(1,128)S(1)}, f32[1,512]{1,0:T(1,128)S(1)}, u32[]{:S(2)}, u32[]{:S(2)}) collective-permute-start(f32[1,512]{1,0:T(1,128)S(1)} %get-tuple-element.110), channel_id=1, source_target_pairs={{0,4},{4,8},{8,12},{12,16},{16,20},{20,24},{24,28},{1,5},{5,9},{9,... | collective-permute-start | bytes 6152 | tf_op jit(solution)/shard_map/ppermute | solution.py:21
  627.4 7.2 collective-permute-start.13
  628.7 5.9 collective-permute-start.14
  633.2 5.5 collective-permute-start.15
  704.4 7.0 collective-permute-start.16
  705.7 5.7 collective-permute-start.17
  707.0 4.5 collective-permute-start.18
  710.1 5.5 collective-permute-start.19
  783.7 7.2 collective-permute-start.20
  785.0 5.9 collective-permute-start.21
  786.3 4.6 collective-permute-start.22
  789.6 5.5 collective-permute-start.23
  (1 other events, 0.9 us)
where the time goes:
time: 853 us; the launch traced here: 842 us
  other arithmetic  494 us (58%)
  blocking collectives  130 us (15%)
  matrix products  90.1 us (11%)
  starting transfers between devices  55.8 us (7%)
  local copies, waits for them, and re-layouts  38.9 us (5%)
  waiting for transfers between devices  25.2 us (3%)
    another operation x16, other arithmetic, body(): factors = jnp.linalg.cholesky(jnp.where(alive_blocks, summed, identity))  314 us
    another operation x25, other arithmetic, solve_factor(): jax.scipy.linalg.solve_triangular(factors, middle, lower=True, trans=1)  163 us
    psum x2, blocking collectives, residual_dot(): return lax.psum(0.5 * jnp.sum(residual * precond_res), ('sx', 'sy'))  86.8 us
    psum x1, blocking collectives, body(): lax.psum(0.5 * jnp.sum(direction * image), ('sx', 'sy'))  42.8 us
    ppermute x12, starting transfers between devices, extended(): before = lax.ppermute(last, axis, up)  40.4 us
    another operation x28, matrix products, solve_factor(): jax.scipy.linalg.solve_triangular(factors, middle, lower=True, trans=1)  26.3 us
    another operation x28, matrix products, solve_factor(): jax.scipy.linalg.solve_triangular(factors, vectors[..., None], lower=True)  26.2 us
    ppermute x12, waiting for transfers between devices, extended(): after = lax.ppermute(initial, axis, down)  23.5 us
  transfers between devices with their start and end apart: 24, of which 9 were waited for; matrix products, arithmetic and copies ran while one was open for 0% of the time, Pallas kernels for 0%

commit v1 on v0

v1 whole, which is shorter than its diff:
```python
import functools

import jax
import jax.numpy as jnp
from jax import lax
from jax.experimental import pallas as pl
from jax.experimental.pallas import tpu as pltpu
from jax.sharding import PartitionSpec as P

ITERS = 2
B = 128
G = 8
MESH = pl.DeviceIdType.MESH
f32 = jnp.float32
bf16 = jnp.bfloat16


def pieces(x):
    h = x.astype(bf16).astype(f32)
    x = x - h
    m = x.astype(bf16).astype(f32)
    return h, m, (x - m).astype(bf16).astype(f32)


LHS_ORDER = (0, 0, 1, 1, 0, 2)
RHS_ORDER = (0, 1, 0, 1, 2, 0)


def stacked(x, order, axis):
    parts = pieces(x)
    return jnp.concatenate([parts[i] for i in order], axis=axis).astype(bf16)


def contract(lhs, rhs, lhs_dim, rhs_dim):
    return lax.dot_general(
        lhs, rhs, (((lhs_dim,), (rhs_dim,)), ((), ())), preferred_element_type=f32
    )


def leaf_sweep(d_ref):
    faces = d_ref.shape[0]
    lane = lax.broadcasted_iota(jnp.int32, (faces, G, B), 2)
    sub = lax.broadcasted_iota(jnp.int32, (faces, G, B), 1)
    wide = lax.broadcasted_iota(jnp.int32, (B, B), 1)

    def group(g, carry):
        base = pl.multiple_of(g * G, G)
        rows = d_ref[:, pl.ds(base, G), :]
        back = lax.rem(B - base, B)
        w = jnp.stack([pltpu.roll(rows[f], back, 1) for f in range(faces)])
        for j in range(G):
            col = w[:, :, j : j + 1]
            row = w[:, j : j + 1, :]
            inv = 1.0 / w[:, j : j + 1, j : j + 1]
            here = lane == j
            r = jnp.where(here[:, :1], 1.0, row) * inv
            w = jnp.where(sub == j, r, jnp.where(here, 0.0, w) - col * r)
        w = jnp.where(lane < G, -w, w)
        w = [pltpu.roll(w[f], base, 1) for f in range(faces)]
        mine = (wide >= base) & (wide < base + G)
        for f in range(faces):
            left = stacked(rows[f], LHS_ORDER, 0)
            right = stacked(w[f], RHS_ORDER, 0)
            d_ref[f] = jnp.where(mine, 0.0, d_ref[f]) - contract(left, right, 0, 0)
        for f in range(faces):
            d_ref[f, pl.ds(base, G), :] = w[f]
        return carry

    lax.fori_loop(0, B // G, group, 0)


def invert_kernel(live_ref, *refs):
    inv_ref, a_ref, d_ref = refs[-3:]
    faces, n, _ = a_ref.shape
    own, part = refs[:faces], refs[faces : 2 * faces]
    for f in range(faces):
        eye = (
            lax.broadcasted_iota(jnp.int32, (n, n), 0)
            == lax.broadcasted_iota(jnp.int32, (n, n), 1)
        ).astype(f32)
        summed = own[f][...].astype(f32) + part[f][...].astype(f32)
        summed = 0.5 * (summed + summed.T)
        a_ref[f] = jnp.where(live_ref[f] > 0, summed, eye)

    def stage(s, carry):
        base = pl.multiple_of(s * B, B)
        d_ref[...] = a_ref[:, pl.ds(base, B), pl.ds(base, B)]
        leaf_sweep(d_ref)

        def face(f, carry):
            neg = d_ref[f]
            rows = a_ref[f, pl.ds(base, B), :]
            cols = a_ref[f, :, pl.ds(base, B)]
            w = -contract(
                stacked(neg, LHS_ORDER, 1), stacked(rows, RHS_ORDER, 0), 1, 0
            )
            a_ref[f, pl.ds(base, B), :] = w
            a_ref[f, pl.ds(base, B), pl.ds(base, B)] = neg
            w = a_ref[f, pl.ds(base, B), :]
            left = stacked(cols, LHS_ORDER, 1)
            right = stacked(w, RHS_ORDER, 0)
            half = n // 2
            for h in range(2):
                lane = lax.broadcasted_iota(jnp.int32, (n, half), 1) + h * half
                mine = (lane >= base) & (lane < base + B)
                old = a_ref[f, :, h * half : (h + 1) * half]
                a_ref[f, :, h * half : (h + 1) * half] = jnp.where(
                    mine, 0.0, old
                ) - contract(left, right[:, h * half : (h + 1) * half], 1, 0)
            a_ref[f, pl.ds(base, B), :] = w
            return carry

        lax.fori_loop(0, faces, face, 0)
        return carry

    lax.fori_loop(0, n // B, stage, 0)
    for f in range(faces):
        for i, piece in enumerate(pieces(-a_ref[f])):
            inv_ref[i, f] = piece.astype(bf16)


def cg_kernel(
    nx, ny, live_ref, slot_ref, rhs_ref, inv_ref, diag_ref, coup_ref,
    sol_ref, res_ref,
    send_buf, recv_buf, xbuf, ybuf, vs_sem, vr_sem, xs_sem, xr_sem, ys_sem, yr_sem,
):
    mx, my = lax.axis_index("sx"), lax.axis_index("sy")
    faces, n = rhs_ref.shape
    recv_buf[...] = jnp.zeros_like(recv_buf)
    send_buf[...] = jnp.zeros_like(send_buf)

    barrier = pltpu.get_barrier_semaphore()
    for o in range(1, nx):
        pl.semaphore_signal(
            barrier, inc=1, device_id={"sx": lax.rem(mx + o, nx), "sy": my}, device_id_type=MESH
        )
    for o in range(1, ny):
        pl.semaphore_signal(
            barrier, inc=1, device_id={"sx": mx, "sy": lax.rem(my + o, ny)}, device_id_type=MESH
        )
    pl.semaphore_wait(barrier, nx + ny - 2)

    sub = lax.broadcasted_iota(jnp.int32, (8, n), 0)
    alive = jnp.zeros((8, n), jnp.bool_)
    slots = jnp.full((8, n), -1, jnp.int32)
    for d in range(faces):
        alive = alive | ((sub == d) & (live_ref[d] > 0))
        slots = jnp.where(sub == d, slot_ref[d], slots)

    guards = (mx > 0, mx < nx - 1, my > 0, my < ny - 1)
    targets = (
        {"sx": mx - 1, "sy": my},
        {"sx": mx + 1, "sy": my},
        {"sx": mx, "sy": my - 1},
        {"sx": mx, "sy": my + 1},
    )

    def vector_copy(phase, d):
        return pltpu.make_async_remote_copy(
            src_ref=send_buf.at[phase, d],
            dst_ref=recv_buf.at[phase, d ^ 1],
            send_sem=vs_sem.at[phase, d],
            recv_sem=vr_sem.at[phase, d ^ 1],
            device_id=targets[d],
            device_id_type=MESH,
        )

    def swap_start(phase, field):
        for d in range(faces):
            send_buf[phase, d, 0:1, :] = field[d : d + 1]

            @pl.when(guards[d])
            def _():
                vector_copy(phase, d).start()

    def swap_finish(phase, field):
        for d in range(faces):

            @pl.when(guards[d])
            def _():
                vector_copy(phase, d).wait_send()
                pltpu.make_async_remote_copy(
                    src_ref=send_buf.at[phase, d ^ 1],
                    dst_ref=recv_buf.at[phase, d],
                    send_sem=vs_sem.at[phase, d ^ 1],
                    recv_sem=vr_sem.at[phase, d],
                    device_id=targets[d],
                    device_id_type=MESH,
                ).wait_recv()

        for d in range(faces):
            field = jnp.where(sub == d, field + recv_buf[phase, d, 0:1, :], field)
        return jnp.where(alive, field, 0.0)

    def ring_copy(buf, send, recv, phase, me, peer, o, device):
        return pltpu.make_async_remote_copy(
            src_ref=buf.at[phase, me],
            dst_ref=buf.at[phase, me],
            send_sem=send.at[phase, o],
            recv_sem=recv.at[phase, me],
            device_id=device,
            device_id_type=MESH,
        )

    def gather_all(buf, send, recv, phase, tile, size, me, device):
        buf[phase, me] = tile
        for o in range(1, size):
            peer = lax.rem(me + o, size)
            ring_copy(buf, send, recv, phase, me, peer, o, device(peer)).start()

    def gather_end(buf, send, recv, phase, size, me, device):
        for o in range(1, size):
            peer = lax.rem(me + o, size)
            ring_copy(buf, send, recv, phase, me, peer, o, device(peer)).wait_send()
            pltpu.make_async_remote_copy(
                src_ref=buf.at[phase, peer],
                dst_ref=buf.at[phase, peer],
                send_sem=send.at[phase, o],
                recv_sem=recv.at[phase, peer],
                device_id=device(peer),
                device_id_type=MESH,
            ).wait_recv()
        return jnp.sum(buf[phase], axis=0)

    def reduce_start(phase, products):
        tile = jnp.zeros((8, B), f32)
        row = lax.broadcasted_iota(jnp.int32, (8, B), 0)
        for q, prod in enumerate(products):
            part = sum(prod[:, i * B : (i + 1) * B] for i in range(n // B))
            tile = jnp.where(row == q, jnp.sum(part, axis=0, keepdims=True), tile)
        gather_all(
            xbuf, xs_sem, xr_sem, phase, tile, nx, mx, lambda p: {"sx": p, "sy": my}
        )

    def reduce_finish(phase, count):
        tile = gather_end(xbuf, xs_sem, xr_sem, phase, nx, mx, lambda p: {"sx": p, "sy": my})
        gather_all(ybuf, ys_sem, yr_sem, phase, tile, ny, my, lambda p: {"sx": mx, "sy": p})
        tile = gather_end(ybuf, ys_sem, yr_sem, phase, ny, my, lambda p: {"sx": mx, "sy": p})
        total = jnp.sum(tile, axis=1, keepdims=True)
        return [total[q : q + 1] for q in range(count)]

    def lifted(field):
        return jnp.concatenate(pieces(field), axis=0).astype(bf16)

    def gathered(out):
        return out[0:8] + out[8:16] + out[16:24]

    def per_face(left, matrices):
        total = jnp.zeros((8, n), f32)
        for d in range(faces):
            out = sum(gathered(contract(left, m, 1, 0)) for m in matrices(d))
            total = jnp.where(sub == d, out, total)
        return total

    def apply_inverse(field):
        return per_face(lifted(field), lambda d: [inv_ref[i, d] for i in range(3)])

    def local_term(field, with_diag):
        field = jnp.where(alive, field, 0.0)
        panel = jnp.zeros((8, n), f32)
        for d in range(faces):
            panel = jnp.where(sub == slot_ref[d], field[d : d + 1], panel)
        left = lifted(panel)
        terms = jnp.zeros((8, n), f32)
        for p in range(faces - 1):
            up = gathered(contract(left, coup_ref[p], 1, 1))
            down = gathered(contract(left, coup_ref[p], 1, 0))
            terms = terms + jnp.where(sub == p, up[p + 1 : p + 2], 0.0)
            terms = terms + jnp.where(sub == p + 1, down[p : p + 1], 0.0)
        if with_diag:
            for p in range(faces):
                out = gathered(contract(left, diag_ref[p], 1, 1))
                terms = terms + jnp.where(sub == p, out, 0.0)
        back = jnp.zeros((8, n), f32)
        for p in range(faces):
            back = jnp.where(slots == p, terms[p : p + 1], back)
        return jnp.where(alive, back, 0.0)

    def precondition(phase, field):
        first = apply_inverse(field)
        spread = local_term(first, False)
        swap_start(phase, spread)
        spread = swap_finish(phase, spread)
        return jnp.where(alive, apply_inverse(field - spread), 0.0)

    source = jnp.concatenate([rhs_ref[...], jnp.zeros((8 - faces, n), f32)], axis=0)
    swap_start(0, source)
    residual = swap_finish(0, source)
    solution = jnp.zeros_like(residual)
    for it in range(ITERS):
        z = precondition(1 + 2 * it, residual)
        term = local_term(z, True)
        swap_start(2 + 2 * it, term)
        products = [0.5 * residual * z, z * term]
        if it:
            products += [z * term_sum + direction * term]
        reduce_start(it, products)
        sums = reduce_finish(it, len(products))
        image_z = swap_finish(2 + 2 * it, term)
        if it == 0:
            rho, curve = sums
            direction, image, term_sum = z, image_z, term
        else:
            new, own, cross = sums
            beta = new / rho
            curve = own + beta * (cross + beta * curve)
            direction = z + beta * direction
            image = image_z + beta * image
            term_sum = term + beta * term_sum
            rho = new
        alpha = rho / curve
        solution = solution + alpha * direction
        residual = residual - alpha * image
    sol_ref[...] = solution[0:faces]
    res_ref[...] = residual[0:faces]


def trade_blocks(blocks):
    nx, ny = lax.axis_size("sx"), lax.axis_size("sy")
    right = [(i, i + 1) for i in range(nx - 1)]
    upper = [(i, i + 1) for i in range(ny - 1)]
    west = lax.ppermute(blocks[1], "sx", right)
    east = lax.ppermute(blocks[0], "sx", [(j, i) for i, j in right])
    south = lax.ppermute(blocks[3], "sy", upper)
    north = lax.ppermute(blocks[2], "sy", [(j, i) for i, j in upper])
    return west, east, south, north


def body(nx, ny, schur_diag, coupling, right_side, face_link, face_start):
    blocks, linked, source = schur_diag[0, 0], coupling[0, 0], right_side[0, 0]
    faces, n, _ = blocks.shape
    live = face_link[0, 0]
    slots = face_start[0, 0] // n
    own = [lax.dynamic_index_in_dim(blocks, slots[d], 0, False) for d in range(faces)]
    partner = trade_blocks(own)
    vmem = pl.BlockSpec(memory_space=pltpu.VMEM)
    smem = pl.BlockSpec(memory_space=pltpu.SMEM)
    inverses = pl.pallas_call(
        invert_kernel,
        out_shape=jax.ShapeDtypeStruct((3, faces, n, n), bf16),
        in_specs=[smem] + [vmem] * (2 * faces),
        out_specs=vmem,
        scratch_shapes=[
            pltpu.VMEM((faces, n, n), f32),
            pltpu.VMEM((faces, B, B), f32),
        ],
        compiler_params=pltpu.CompilerParams(vmem_limit_bytes=48 * 2**20),
    )(live, *own, *partner)
    phases = 1 + 2 * ITERS
    sol, res = pl.pallas_call(
        functools.partial(cg_kernel, nx, ny),
        out_shape=[jax.ShapeDtypeStruct((faces, n), f32)] * 2,
        in_specs=[smem, smem] + [vmem] * 4,
        out_specs=[vmem, vmem],
        scratch_shapes=[
            pltpu.VMEM((phases, faces, 8, n), f32),
            pltpu.VMEM((phases, faces, 8, n), f32),
            pltpu.VMEM((ITERS, nx, 8, B), f32),
            pltpu.VMEM((ITERS, ny, 8, B), f32),
            pltpu.SemaphoreType.DMA((phases, faces)),
            pltpu.SemaphoreType.DMA((phases, faces)),
            pltpu.SemaphoreType.DMA((ITERS, nx)),
            pltpu.SemaphoreType.DMA((ITERS, nx)),
            pltpu.SemaphoreType.DMA((ITERS, ny)),
            pltpu.SemaphoreType.DMA((ITERS, ny)),
        ],
        compiler_params=pltpu.CompilerParams(
            collective_id=0, has_side_effects=True, vmem_limit_bytes=48 * 2**20
        ),
    )(live, slots, source, inverses, blocks, linked)
    return sol[None, None], res[None, None]


def solution(mesh):
    shape = dict(mesh.shape)
    return jax.shard_map(
        functools.partial(body, shape["sx"], shape["sy"]),
        mesh=mesh,
        in_specs=(
            P("sy", "sx", None, None, None),
            P("sy", "sx", None, None, None),
            P("sy", "sx", None, None),
            P("sy", "sx", None),
            P("sy", "sx", None),
        ),
        out_specs=(P("sy", "sx", None, None), P("sy", "sx", None, None)),
        check_vma=False,
    )
```

time: 853 us -> 155 us (0.18); the launches traced: 842 us -> 155 us
  other arithmetic: 494 us -> 0.66 us
  blocking collectives: 130 us -> 0 us
  Pallas kernels: 0 us -> 122 us
  matrix products: 90.1 us -> 0 us
  starting transfers between devices: 55.8 us -> 9.04 us
  local copies, waits for them, and re-layouts: 38.9 us -> 3.5 us
  waiting for transfers between devices: 25.2 us -> 11.2 us
    another operation x61 -> x0, other arithmetic: 478 us -> none  [the longest x16 314 us: body(): factors = jnp.linalg.cholesky(jnp.where(alive_blocks, summed, identity))]
    psum x3 -> x0, blocking collectives: 130 us -> none  [the longest x2 86.8 us: residual_dot(): return lax.psum(0.5 * jnp.sum(residual * precond_res), ('sx', 'sy'))]
    pallas_call x0 -> x2, Pallas kernels: none -> 122 us  [the longest x1 80.6 us: body(): pl.pallas_call(invert_kernel, out_shape=jax.ShapeDtypeStruct((3, faces, n...]
    another operation x62 -> x0, matrix products: 67.3 us -> none  [the longest x28 26.3 us: solve_factor(): jax.scipy.linalg.solve_triangular(factors, middle, lower=True, trans=1)]
    ppermute x24 -> x4, starting transfers between devices: 55.8 us -> 9.04 us  [the longest x1 4.96 us: trade_blocks(): south = lax.ppermute(blocks[3], 'sy', upper)]
    dot_general x10 -> x0, matrix products: 22.9 us -> none  [the longest x4 10.9 us: panel_terms(): jnp.einsum('...pij,...pj->...pi', linked, vectors[..., 1:, :], precision=...]
    another operation x22 -> x0, local copies, waits for them, and re-layouts: 18.4 us -> none  [the longest x13 15.1 us: solve_factor(): jax.scipy.linalg.solve_triangular(factors, middle, lower=True, trans=1)]
    ppermute x24 -> x4, waiting for transfers between devices: 25.2 us -> 11.2 us  [the longest x1 7.03 us: trade_blocks(): south = lax.ppermute(blocks[3], 'sy', upper)]
  transfers between devices with their start and end apart: 24 -> 4, of which waited for: 9 -> 2; matrix products, arithmetic and copies ran while one was open for 0% -> 0% of each run, Pallas kernels for 0% -> 0%
where the time goes in v1:
time: 155 us
  Pallas kernels  122 us (79%)
  waiting for transfers between devices  11.2 us (7%)
  starting transfers between devices  9.04 us (6%)
  between operations  8.36 us (5%)
  local copies, waits for them, and re-layouts  3.5 us (2%)
    pallas_call x1, Pallas kernels, body(): pl.pallas_call(invert_kernel, out_shape=jax.ShapeDtypeStruct((3, faces, n...  80.6 us
    pallas_call x1, Pallas kernels, body(): pl.pallas_call(functools.partial(cg_kernel, nx, ny), out_shape=[jax.Shape...  41.6 us
    ppermute x1, waiting for transfers between devices, trade_blocks(): south = lax.ppermute(blocks[3], 'sy', upper)  7.03 us
    ppermute x1, starting transfers between devices, trade_blocks(): south = lax.ppermute(blocks[3], 'sy', upper)  4.96 us
    ppermute x1, waiting for transfers between devices, trade_blocks(): north = lax.ppermute(blocks[2], 'sy', [(j, i) for i, j in upper])  4.15 us
  transfers between devices with their start and end apart: 4, of which 2 were waited for; matrix products, arithmetic and copies ran while one was open for 0% of the time, Pallas kernels for 0%

profile of v1, /device:TPU:0, one launch (start us, length us, event | category | flops | bytes accessed | tf_op | source)
XLA Modules:
  0.0 155.0 jit_solution(16077456214699779216)
XLA Ops:
  0.6 0.7 and_select_fusion.slot_ref
  1.3 0.6 fusion
  9.6 0.0 copy-start.3
  9.6 1.7 %dynamic-slice_bitcast_fusion = (bf16[512,512]{1,0:T(8,128)(2,1)S(1)}, bf16[512,512]{1,0:T(8,128)(2,1)S(1)}, bf16[512,512]{1,0:T(8,128)(2,1)S(1)}, bf16[512,512]{1,0:T(8,128)(2,1)S(1)}) fusion(bf16[1,1,4,512,512]{4,3,2,1,0:T(8,128)(2,1)} %param.5, s32[]{:T(128)S(6)} %select_n.22, s32[]{:T(128)S(6)} %select_n.21, s32[]{:T(128)S(6)} %select_n.20, s32[]{:T(128)S(6)} %select_n.19), kind=kLoop, calls=%fused_computation | loop fusion | bytes 4194320 | tf_op jit(solution)/shard_map/jit(dynamic_index_in_dim)/squeeze | solution.py:334
  11.2 5.0 %collective-permute-start.2 = (bf16[512,512]{1,0:T(8,128)(2,1)S(1)}, bf16[512,512]{1,0:T(8,128)(2,1)S(1)}, u32[]{:S(2)}, u32[]{:S(2)}) collective-permute-start(bf16[512,512]{1,0:T(8,128)(2,1)S(1)} %get-tuple-element.6.refs_3_), channel_id=1, source_target_pairs={{0,1},{1,2},{2,3},{4,5},{5,6},{6,7},{8,9},{9,10},{10,11},{12,13},{... | collective-permute-start | bytes 1572872 | tf_op jit(solution)/shard_map/ppermute | solution.py:324
  16.2 1.3 collective-permute-start.3
  17.5 1.5 collective-permute-start
  19.0 1.3 collective-permute-start.1
  20.3 7.0 %collective-permute-done.2.refs_6_ = bf16[512,512]{1,0:T(8,128)(2,1)S(1)} collective-permute-done((bf16[512,512]{1,0:T(8,128)(2,1)S(1)}, bf16[512,512]{1,0:T(8,128)(2,1)S(1)}, u32[]{:S(2)}, u32[]{:S(2)}) %collective-permute-start.2) | collective-permute-done | bytes 524320 | tf_op jit(solution)/shard_map/ppermute | solution.py:324
  27.3 4.1 %collective-permute-done.3.refs_7_ = bf16[512,512]{1,0:T(8,128)(2,1)S(1)} collective-permute-done((bf16[512,512]{1,0:T(8,128)(2,1)S(1)}, bf16[512,512]{1,0:T(8,128)(2,1)S(1)}, u32[]{:S(2)}, u32[]{:S(2)}) %collective-permute-start.3) | collective-permute-done | bytes 524320 | tf_op jit(solution)/shard_map/ppermute | solution.py:325
  31.5 0.0 collective-permute-done.refs_4_
  31.5 0.0 collective-permute-done.1.refs_5_
  31.5 0.0 copy-done.3
  31.5 0.0 copy-start
  31.5 0.0 copy-start.1
  31.5 0.0 copy-start.2
  31.5 80.6 %shard_map.68.inv_ref = bf16[3,4,512,512]{3,2,1,0:T(8,128)(2,1)} custom-call(s32[4]{0:T(128)S(1)} %bitcast.31, bf16[512,512]{1,0:T(8,128)(2,1)S(1)} %get-tuple-element.9.refs_0_, bf16[512,512]{1,0:T(8,128)(2,1)S(1)} %get-tuple-element.8.refs_1_, bf16[512,512]{1,0:T(8,128)(2,1)S(1)} %get-tuple-element.7.refs_2_, ...), custom_call_target="tpu_custom_call" | custom-call | tf_op jit(solution)/shard_map/pallas_call | solution.py:338
  112.2 0.0 copy-done
  112.2 0.0 copy-done.1
  112.2 0.0 copy-done.2
  112.2 41.6 %shard_map.69 = (f32[4,512]{1,0:T(4,128)S(1)}, f32[4,512]{1,0:T(4,128)S(1)}) custom-call(s32[4]{0:T(128)S(1)} %bitcast.32, s32[4]{0:T(128)S(1)} %and_select_fusion.slot_ref, f32[4,512]{1,0:T(4,128)S(1)} %bitcast.30, bf16[3,4,512,512]{3,2,1,0:T(8,128)(2,1)} %shard_map.68.inv_ref, bf16[4,512,512]{2,1,0:T(8,128)(2,1)S(1)} %bitcast.26, ...), custom_call_target="tpu_custom_call" | custom-call | tf_op jit(solution)/shard_map/pallas_call | solution.py:350
  153.8 0.6 copy.9
  154.4 0.6 copy.10
Async XLA Ops:
  9.6 21.9 %copy-start.3 = (s32[1,1,4]{2,1,0:T(1,128)S(1)}, s32[1,1,4]{2,1,0:T(1,128)}, u32[]{:S(2)}) copy-start(s32[1,1,4]{2,1,0:T(1,128)} %param.8) | copy-start | bytes 52
  11.2 16.1 %collective-permute-start.2 = (bf16[512,512]{1,0:T(8,128)(2,1)S(1)}, bf16[512,512]{1,0:T(8,128)(2,1)S(1)}, u32[]{:S(2)}, u32[]{:S(2)}) collective-permute-start(bf16[512,512]{1,0:T(8,128)(2,1)S(1)} %get-tuple-element.6.refs_3_), channel_id=1, source_target_pairs={{0,1},{1,2},{2,3},{4,5},{5,6},{6,7},{8,9},{9,10},{10,11},{12,13},{... | collective-permute-start | bytes 1572872 | tf_op jit(solution)/shard_map/ppermute | solution.py:324
  16.2 15.3 %collective-permute-start.3 = (bf16[512,512]{1,0:T(8,128)(2,1)S(1)}, bf16[512,512]{1,0:T(8,128)(2,1)S(1)}, u32[]{:S(2)}, u32[]{:S(2)}) collective-permute-start(bf16[512,512]{1,0:T(8,128)(2,1)S(1)} %get-tuple-element.7.refs_2_), channel_id=1, source_target_pairs={{1,0},{2,1},{3,2},{5,4},{6,5},{7,6},{9,8},{10,9},{11,10},{13,12},{... | collective-permute-start | bytes 1572872 | tf_op jit(solution)/shard_map/ppermute | solution.py:325
  17.5 14.0 %collective-permute-start = (bf16[512,512]{1,0:T(8,128)(2,1)S(1)}, bf16[512,512]{1,0:T(8,128)(2,1)S(1)}, u32[]{:S(2)}, u32[]{:S(2)}) collective-permute-start(bf16[512,512]{1,0:T(8,128)(2,1)S(1)} %get-tuple-element.8.refs_1_), channel_id=1, source_target_pairs={{0,4},{4,8},{8,12},{12,16},{16,20},{20,24},{24,28},{1,5},{5,9},{9,... | collective-permute-start | bytes 1572872 | tf_op jit(solution)/shard_map/ppermute | solution.py:322
  19.0 12.5 %collective-permute-start.1 = (bf16[512,512]{1,0:T(8,128)(2,1)S(1)}, bf16[512,512]{1,0:T(8,128)(2,1)S(1)}, u32[]{:S(2)}, u32[]{:S(2)}) collective-permute-start(bf16[512,512]{1,0:T(8,128)(2,1)S(1)} %get-tuple-element.9.refs_0_), channel_id=1, source_target_pairs={{4,0},{8,4},{12,8},{16,12},{20,16},{24,20},{28,24},{5,1},{9,5},{13... | collective-permute-start | bytes 1572872 | tf_op jit(solution)/shard_map/ppermute | solution.py:323
  31.5 80.7 %copy-start = (bf16[1,1,4,512,512]{4,3,2,1,0:T(8,128)(2,1)S(1)}, bf16[1,1,4,512,512]{4,3,2,1,0:T(8,128)(2,1)}, u32[]{:S(2)}) copy-start(bf16[1,1,4,512,512]{4,3,2,1,0:T(8,128)(2,1)} %param.5) | copy-start | bytes 6291460
  31.5 80.7 %copy-start.1 = (bf16[1,1,3,512,512]{4,3,2,1,0:T(8,128)(2,1)S(1)}, bf16[1,1,3,512,512]{4,3,2,1,0:T(8,128)(2,1)}, u32[]{:S(2)}) copy-start(bf16[1,1,3,512,512]{4,3,2,1,0:T(8,128)(2,1)} %param.6) | copy-start | bytes 4718596
  31.5 80.7 %copy-start.2 = (f32[1,1,4,512]{3,2,1,0:T(4,128)S(1)}, f32[1,1,4,512]{3,2,1,0:T(4,128)}, u32[]{:S(2)}) copy-start(f32[1,1,4,512]{3,2,1,0:T(4,128)} %param.7) | copy-start | bytes 24580

commit v2 on v1

--- a/solution.py
+++ b/solution.py
@@ -49,9 +49,9 @@
         back = lax.rem(B - base, B)
         w = jnp.stack([pltpu.roll(rows[f], back, 1) for f in range(faces)])
         for j in range(G):
-            col = w[:, :, j : j + 1]
+            col = jnp.broadcast_to(w[:, :, j : j + 1], w.shape)
             row = w[:, j : j + 1, :]
-            inv = 1.0 / w[:, j : j + 1, j : j + 1]
+            inv = pl.reciprocal(col[:, j : j + 1, :], approx=False)
             here = lane == j
             r = jnp.where(here[:, :1], 1.0, row) * inv
             w = jnp.where(sub == j, r, jnp.where(here, 0.0, w) - col * r)

time: 155 us -> 155 us (level)
  no operation moved by 1% of the time
where the time goes in v2:
time: 155 us; the launch traced here: 154 us
  Pallas kernels  122 us (79%)
  waiting for transfers between devices  11.2 us (7%)
  starting transfers between devices  9.04 us (6%)
  between operations  8.36 us (5%)
  local copies, waits for them, and re-layouts  3.5 us (2%)
    pallas_call x1, Pallas kernels, body(): pl.pallas_call(invert_kernel, out_shape=jax.ShapeDtypeStruct((3, faces, n...  79.9 us
    pallas_call x1, Pallas kernels, body(): pl.pallas_call(functools.partial(cg_kernel, nx, ny), out_shape=[jax.Shape...  41.6 us
    ppermute x1, waiting for transfers between devices, trade_blocks(): south = lax.ppermute(blocks[3], 'sy', upper)  7.03 us
    ppermute x1, starting transfers between devices, trade_blocks(): south = lax.ppermute(blocks[3], 'sy', upper)  4.96 us
    ppermute x1, waiting for transfers between devices, trade_blocks(): north = lax.ppermute(blocks[2], 'sy', [(j, i) for i, j in upper])  4.15 us
  transfers between devices with their start and end apart: 4, of which 2 were waited for; matrix products, arithmetic and copies ran while one was open for 0% of the time, Pallas kernels for 0%

profile of v2, /device:TPU:0, one launch (start us, length us, event | category | flops | bytes accessed | tf_op | source)
XLA Modules:
  0.0 154.3 jit_solution(18248308203758772447)
XLA Ops:
  0.6 0.7 and_select_fusion.slot_ref
  1.3 0.6 fusion
  9.6 0.0 copy-start.3
  9.6 1.7 %dynamic-slice_bitcast_fusion = (bf16[512,512]{1,0:T(8,128)(2,1)S(1)}, bf16[512,512]{1,0:T(8,128)(2,1)S(1)}, bf16[512,512]{1,0:T(8,128)(2,1)S(1)}, bf16[512,512]{1,0:T(8,128)(2,1)S(1)}) fusion(bf16[1,1,4,512,512]{4,3,2,1,0:T(8,128)(2,1)} %param.5, s32[]{:T(128)S(6)} %select_n.22, s32[]{:T(128)S(6)} %select_n.21, s32[]{:T(128)S(6)} %select_n.20, s32[]{:T(128)S(6)} %select_n.19), kind=kLoop, calls=%fused_computation | loop fusion | bytes 4194320 | tf_op jit(solution)/shard_map/jit(dynamic_index_in_dim)/squeeze | solution.py:334
  11.2 5.0 %collective-permute-start.2 = (bf16[512,512]{1,0:T(8,128)(2,1)S(1)}, bf16[512,512]{1,0:T(8,128)(2,1)S(1)}, u32[]{:S(2)}, u32[]{:S(2)}) collective-permute-start(bf16[512,512]{1,0:T(8,128)(2,1)S(1)} %get-tuple-element.6.refs_3_), channel_id=1, source_target_pairs={{0,1},{1,2},{2,3},{4,5},{5,6},{6,7},{8,9},{9,10},{10,11},{12,13},{... | collective-permute-start | bytes 1572872 | tf_op jit(solution)/shard_map/ppermute | solution.py:324
  16.2 1.3 collective-permute-start.3
  17.5 1.5 collective-permute-start
  19.0 1.3 collective-permute-start.1
  20.3 7.0 %collective-permute-done.2.refs_6_ = bf16[512,512]{1,0:T(8,128)(2,1)S(1)} collective-permute-done((bf16[512,512]{1,0:T(8,128)(2,1)S(1)}, bf16[512,512]{1,0:T(8,128)(2,1)S(1)}, u32[]{:S(2)}, u32[]{:S(2)}) %collective-permute-start.2) | collective-permute-done | bytes 524320 | tf_op jit(solution)/shard_map/ppermute | solution.py:324
  27.3 4.1 %collective-permute-done.3.refs_7_ = bf16[512,512]{1,0:T(8,128)(2,1)S(1)} collective-permute-done((bf16[512,512]{1,0:T(8,128)(2,1)S(1)}, bf16[512,512]{1,0:T(8,128)(2,1)S(1)}, u32[]{:S(2)}, u32[]{:S(2)}) %collective-permute-start.3) | collective-permute-done | bytes 524320 | tf_op jit(solution)/shard_map/ppermute | solution.py:325
  31.5 0.0 collective-permute-done.refs_4_
  31.5 0.0 collective-permute-done.1.refs_5_
  31.5 0.0 copy-done.3
  31.5 0.0 copy-start
  31.5 0.0 copy-start.1
  31.5 0.0 copy-start.2
  31.5 79.9 %shard_map.68.inv_ref = bf16[3,4,512,512]{3,2,1,0:T(8,128)(2,1)} custom-call(s32[4]{0:T(128)S(1)} %bitcast.31, bf16[512,512]{1,0:T(8,128)(2,1)S(1)} %get-tuple-element.9.refs_0_, bf16[512,512]{1,0:T(8,128)(2,1)S(1)} %get-tuple-element.8.refs_1_, bf16[512,512]{1,0:T(8,128)(2,1)S(1)} %get-tuple-element.7.refs_2_, ...), custom_call_target="tpu_custom_call" | custom-call | tf_op jit(solution)/shard_map/pallas_call | solution.py:338
  111.5 0.0 copy-done
  111.5 0.0 copy-done.1
  111.5 0.0 copy-done.2
  111.5 41.6 %shard_map.69 = (f32[4,512]{1,0:T(4,128)S(1)}, f32[4,512]{1,0:T(4,128)S(1)}) custom-call(s32[4]{0:T(128)S(1)} %bitcast.32, s32[4]{0:T(128)S(1)} %and_select_fusion.slot_ref, f32[4,512]{1,0:T(4,128)S(1)} %bitcast.30, bf16[3,4,512,512]{3,2,1,0:T(8,128)(2,1)} %shard_map.68.inv_ref, bf16[4,512,512]{2,1,0:T(8,128)(2,1)S(1)} %bitcast.26, ...), custom_call_target="tpu_custom_call" | custom-call | tf_op jit(solution)/shard_map/pallas_call | solution.py:350
  153.1 0.6 copy.9
  153.7 0.6 copy.10
Async XLA Ops:
  9.6 21.9 %copy-start.3 = (s32[1,1,4]{2,1,0:T(1,128)S(1)}, s32[1,1,4]{2,1,0:T(1,128)}, u32[]{:S(2)}) copy-start(s32[1,1,4]{2,1,0:T(1,128)} %param.8) | copy-start | bytes 52
  11.2 16.1 %collective-permute-start.2 = (bf16[512,512]{1,0:T(8,128)(2,1)S(1)}, bf16[512,512]{1,0:T(8,128)(2,1)S(1)}, u32[]{:S(2)}, u32[]{:S(2)}) collective-permute-start(bf16[512,512]{1,0:T(8,128)(2,1)S(1)} %get-tuple-element.6.refs_3_), channel_id=1, source_target_pairs={{0,1},{1,2},{2,3},{4,5},{5,6},{6,7},{8,9},{9,10},{10,11},{12,13},{... | collective-permute-start | bytes 1572872 | tf_op jit(solution)/shard_map/ppermute | solution.py:324
  16.2 15.3 %collective-permute-start.3 = (bf16[512,512]{1,0:T(8,128)(2,1)S(1)}, bf16[512,512]{1,0:T(8,128)(2,1)S(1)}, u32[]{:S(2)}, u32[]{:S(2)}) collective-permute-start(bf16[512,512]{1,0:T(8,128)(2,1)S(1)} %get-tuple-element.7.refs_2_), channel_id=1, source_target_pairs={{1,0},{2,1},{3,2},{5,4},{6,5},{7,6},{9,8},{10,9},{11,10},{13,12},{... | collective-permute-start | bytes 1572872 | tf_op jit(solution)/shard_map/ppermute | solution.py:325
  17.5 14.0 %collective-permute-start = (bf16[512,512]{1,0:T(8,128)(2,1)S(1)}, bf16[512,512]{1,0:T(8,128)(2,1)S(1)}, u32[]{:S(2)}, u32[]{:S(2)}) collective-permute-start(bf16[512,512]{1,0:T(8,128)(2,1)S(1)} %get-tuple-element.8.refs_1_), channel_id=1, source_target_pairs={{0,4},{4,8},{8,12},{12,16},{16,20},{20,24},{24,28},{1,5},{5,9},{9,... | collective-permute-start | bytes 1572872 | tf_op jit(solution)/shard_map/ppermute | solution.py:322
  19.0 12.5 %collective-permute-start.1 = (bf16[512,512]{1,0:T(8,128)(2,1)S(1)}, bf16[512,512]{1,0:T(8,128)(2,1)S(1)}, u32[]{:S(2)}, u32[]{:S(2)}) collective-permute-start(bf16[512,512]{1,0:T(8,128)(2,1)S(1)} %get-tuple-element.9.refs_0_), channel_id=1, source_target_pairs={{4,0},{8,4},{12,8},{16,12},{20,16},{24,20},{28,24},{5,1},{9,5},{13... | collective-permute-start | bytes 1572872 | tf_op jit(solution)/shard_map/ppermute | solution.py:323
  31.5 80.0 %copy-start = (bf16[1,1,4,512,512]{4,3,2,1,0:T(8,128)(2,1)S(1)}, bf16[1,1,4,512,512]{4,3,2,1,0:T(8,128)(2,1)}, u32[]{:S(2)}) copy-start(bf16[1,1,4,512,512]{4,3,2,1,0:T(8,128)(2,1)} %param.5) | copy-start | bytes 6291460
  31.5 80.0 %copy-start.1 = (bf16[1,1,3,512,512]{4,3,2,1,0:T(8,128)(2,1)S(1)}, bf16[1,1,3,512,512]{4,3,2,1,0:T(8,128)(2,1)}, u32[]{:S(2)}) copy-start(bf16[1,1,3,512,512]{4,3,2,1,0:T(8,128)(2,1)} %param.6) | copy-start | bytes 4718596
  31.5 80.0 %copy-start.2 = (f32[1,1,4,512]{3,2,1,0:T(4,128)S(1)}, f32[1,1,4,512]{3,2,1,0:T(4,128)}, u32[]{:S(2)}) copy-start(f32[1,1,4,512]{3,2,1,0:T(4,128)} %param.7) | copy-start | bytes 24580
